TPU v7x, 32 devices: a whole 2x2x4 slice. The times are simulated.
32 devices in a mesh: space: 8 (over z, core), samp: 4 (over y, x).
Axes of the slice: x: 2, y: 2, z: 4, core: 2. Of those that a mesh axis runs over, the one named last changes fastest.
Arguments:
- basis_u: bfloat16 [128, 16, 8, 128], P('samp', 'space'), may hold values from -0.75 to 0.75
- basis_v: bfloat16 [128, 32768], P('space', 'samp'), may hold values from -0.75 to 0.75
- core_s: float32 [128, 128], replicated, may hold values from -4 to 4
- face_class: int32 [6, 16, 8, 128], P(None, 'space'), may hold values from 0 to 3
- sample_class: int32 [32768], P('samp'), may hold values from 0 to 3
Outputs:
- k_new: float32 [128, 16, 8, 128], P('samp', 'space')
- l_new: float32 [128, 32768], P('space', 'samp')
All inputs are finite; a program needn't handle non-finite values.
Results may differ from a plain program's by a relative error of at most 0.0046.
Values may be sent and summed in bfloat16 or wider, within the bound.
A program may use at most 64 MiB of HBM per device.

v0:
```python
import jax
import jax.numpy as jnp
from jax import lax
from jax.sharding import PartitionSpec as P

step_size = 0.1


def padded(cells, sides, width):
    for axis, dim in sides:
        count = lax.axis_size(axis)
        ends = count - 1
        head = lax.slice_in_dim(cells, 0, width, axis=dim)
        tail = lax.slice_in_dim(cells, cells.shape[dim] - width, cells.shape[dim], axis=dim)
        cells = jnp.concatenate(
            [
                lax.ppermute(tail, axis, [(i, (i + 1) % count) for i in range(ends)]),
                cells,
                lax.ppermute(head, axis, [((i + 1) % count, i) for i in range(ends)]),
            ],
            axis=dim,
        )
    return cells


def with_core(factor, core_b):
    rank_size = core_b.shape[0]
    flat_rows = factor.reshape(rank_size, -1)
    product = lax.dot_general(
        core_b, flat_rows, (((0,), (0,)), ((), ())), preferred_element_type=jnp.float32
    ).astype(jnp.bfloat16)
    return product.reshape(factor.shape)


def diffuse(padded_k, face_class):
    weight = 0.25 * jnp.exp2(face_class.astype(jnp.float32))[:, None]
    padded_grid = jnp.pad(padded_k.astype(jnp.float32), ((0, 0), (0, 0), (1, 1), (1, 1)))
    centre = padded_grid[:, 1:-1, 1:-1, 1:-1]
    beside_all = (
        padded_grid[:, :-2, 1:-1, 1:-1],
        padded_grid[:, 2:, 1:-1, 1:-1],
        padded_grid[:, 1:-1, :-2, 1:-1],
        padded_grid[:, 1:-1, 2:, 1:-1],
        padded_grid[:, 1:-1, 1:-1, :-2],
        padded_grid[:, 1:-1, 1:-1, 2:],
    )
    summed = jnp.zeros_like(centre)
    for side_index in range(6):
        summed = summed + weight[side_index] * (beside_all[side_index] - centre)
    return summed


def per_device(basis_u, basis_v, core_s, face_class, sample_class):
    n_space = lax.axis_size("space")
    n_samp = lax.axis_size("samp")
    narrow, depth_x, rows_y, cols_z = basis_u.shape
    rank_size = core_s.shape[0]
    core_b = core_s.astype(jnp.bfloat16)
    full_u = lax.all_gather(basis_u, "samp", axis=0, tiled=True)
    k_old = with_core(full_u, core_b)
    padded_k = padded(k_old, (("space", 1),), 1)
    laplace = diffuse(padded_k, face_class)
    cells_total = depth_x * rows_y * cols_z * n_space
    samp_rows = basis_v.shape[1]
    samples_total = samp_rows * n_samp
    lane_width = rank_size // n_space
    full_v = lax.all_gather(basis_v, "space", axis=0, tiled=True)
    k_flat = k_old.reshape(rank_size, -1)
    u_rows = full_u.reshape(rank_size, -1)
    lap_b = laplace.reshape(rank_size, -1).astype(jnp.bfloat16)
    moment_part = lax.dot_general(
        u_rows, lap_b, (((1,), (1,)), ((), ())), preferred_element_type=jnp.float32
    )
    moment = lax.psum(moment_part, "space")
    growth = 0.5 + 0.5 * sample_class.astype(jnp.float32)
    block_rows = min(256, samp_rows)
    block_count = samp_rows // block_rows
    cell_weight = rank_size / cells_total

    def tile_terms(offset):
        v_block = lax.dynamic_slice_in_dim(full_v, offset, block_rows, 1)
        g_block = lax.dynamic_slice_in_dim(growth, offset, block_rows, 0)
        sample_field = lax.dot_general(
            k_flat, v_block, (((0,), (0,)), ((), ())), preferred_element_type=jnp.float32
        )
        reaction = (
            g_block[None, :] * sample_field - sample_field * sample_field * sample_field
        ).astype(jnp.bfloat16)
        onto_v = lax.dot_general(
            v_block, reaction, (((1,), (1,)), ((), ())), preferred_element_type=jnp.float32
        )
        onto_u = lax.dot_general(
            u_rows, reaction, (((1,), (0,)), ((), ())), preferred_element_type=jnp.float32
        )
        return (onto_v, onto_u * cell_weight)

    start_acc = jnp.zeros((rank_size, k_flat.shape[1]), jnp.float32)

    def turn_after(turn_index, state_pair):
        accumulated, l_terms = state_pair
        offset = turn_index * block_rows
        onto_v, l_term = tile_terms(offset)
        l_terms = lax.dynamic_update_slice_in_dim(l_terms, l_term, offset, 1)
        return (accumulated + onto_v, l_terms)

    start_terms = jnp.zeros((rank_size, samp_rows), jnp.float32)
    accumulated, l_terms = lax.fori_loop(0, block_count, turn_after, (start_acc, start_terms))
    l_proj = lax.psum_scatter(l_terms, "space", scatter_dimension=0, tiled=True)
    samp_offset = lax.axis_index("samp") * narrow
    k_term = accumulated.reshape(rank_size, depth_x, rows_y, cols_z)
    k_proj = lax.psum_scatter(k_term, "samp", scatter_dimension=0, tiled=True)
    k_proj = k_proj * (rank_size / samples_total)
    k_mine = lax.dynamic_slice_in_dim(k_old, samp_offset, narrow, 0).astype(jnp.float32)
    lap_mine = lax.dynamic_slice_in_dim(laplace, samp_offset, narrow, 0)
    k_new = k_mine + step_size * (lap_mine + k_proj)
    lane_offset = lax.axis_index("space") * lane_width
    core_rows = lax.dynamic_slice_in_dim(core_b, lane_offset, lane_width, 0)
    l_old = jnp.dot(core_rows, full_v, preferred_element_type=jnp.float32)
    moment_rows = lax.dynamic_slice_in_dim(moment, lane_offset, lane_width, 0) * cell_weight
    side_term = jnp.dot(moment_rows, full_v.astype(jnp.float32), precision=lax.Precision.HIGHEST)
    l_new = l_old + step_size * (side_term + l_proj)
    return (k_new, l_new)


def solution(mesh):
    placed = (
        P("samp", "space", None, None),
        P("space", "samp"),
        P(),
        P(None, "space", None, None),
        P("samp"),
    )
    return jax.shard_map(
        per_device,
        mesh=mesh,
        in_specs=placed,
        out_specs=(P("samp", "space", None, None), P("space", "samp")),
        check_vma=False,
    )
```

profile of v0, /device:TPU:0, one launch (start us, length us, event | category | flops | bytes accessed | tf_op | source)
XLA Modules:
  0.0 323.6 jit_solution(11626277581168068768)
XLA Ops:
  8.8 11.8 %all_gather.6 = bf16[128,2,8,128]{3,2,1,0:T(8,128)(2,1)S(1)} all-gather(bf16[32,2,8,128]{3,2,1,0:T(8,128)(2,1)} %param.7), channel_id=1, replica_groups=mesh['space'=8,'samp'=4] {'samp'}, dimensions={0}, use_global_device_ids=true | all-gather | bytes 655360 | tf_op jit(solution)/shard_map/all_gather | solution.py:59
  22.7 18.8 %all-gather.2.cloned.1.call-done = bf16[128,8192]{1,0:T(8,128)(2,1)} async-done(((bf16[16,8192]{1,0:T(8,128)(2,1)}), bf16[128,8192]{1,0:T(8,128)(2,1)}) %all-gather.2.cloned.1.call-update) | async-done | bytes 2097168 | tf_op jit(solution)/shard_map/all_gather | solution.py:67
  41.4 2.4 broadcast_in_dim.11.clone
  43.8 134.0 %while.16 = (s32[]{:T(128)}, f32[128,2048]{1,0:T(8,128)S(1)}, f32[128,8192]{1,0:T(8,128)}, bf16[128,8192]{1,0:T(8,128)(2,1)}, f32[8192]{0:T(1024)S(1)}, /*index=...) while((s32[]{:T(128)}, f32[128,2048]{1,0:T(8,128)S(1)}, ...), condition=%wide.region_1.2_spmd.clone, body=%wide.region_0.1_spmd.clone.sunk | while | flops 405831680 | bytes 7081149 | solution.py:107
  43.9 1.6 fusion.58
  45.5 1.3 convolution_add_fusion.3
  48.1 1.6 fusion.58
  49.7 1.3 convolution_add_fusion.3
  52.3 1.6 fusion.58
  53.9 1.3 convolution_add_fusion.3
  56.5 1.6 fusion.58
  58.1 1.3 convolution_add_fusion.3
  60.6 1.6 fusion.58
  64.8 1.6 fusion.58
  69.0 1.6 fusion.58
  70.6 1.3 convolution_add_fusion.3
  73.2 1.6 fusion.58
  74.8 1.3 convolution_add_fusion.3
  77.4 1.6 fusion.58
  79.0 1.3 convolution_add_fusion.3
  81.6 1.6 fusion.58
  85.8 1.6 fusion.58
  87.4 1.3 convolution_add_fusion.3
  90.0 1.6 fusion.58
  91.6 1.3 convolution_add_fusion.3
  94.2 1.6 fusion.58
  98.4 1.6 fusion.58
  102.6 1.6 fusion.58
  106.8 1.6 fusion.58
  110.9 1.6 fusion.58
  115.1 1.6 fusion.58
  116.7 1.3 convolution_add_fusion.3
  119.3 1.6 fusion.58
  120.9 1.3 convolution_add_fusion.3
  123.5 1.6 fusion.58
  125.1 1.3 convolution_add_fusion.3
  127.7 1.6 fusion.58
  131.8 1.6 fusion.58
  133.4 1.3 convolution_add_fusion.3
  136.0 1.6 fusion.58
  137.6 1.3 convolution_add_fusion.3
  140.2 1.6 fusion.58
  141.8 1.3 convolution_add_fusion.3
  144.4 1.6 fusion.58
  146.0 1.3 convolution_add_fusion.3
  148.6 1.6 fusion.58
  150.2 1.3 convolution_add_fusion.3
  152.7 1.6 fusion.58
  154.3 1.3 convolution_add_fusion.3
  156.9 1.6 fusion.58
  158.5 1.3 convolution_add_fusion.3
  161.1 1.6 fusion.58
  165.3 1.6 fusion.58
  169.5 1.6 fusion.58
  171.1 1.3 convolution_add_fusion.3
  173.7 1.6 fusion.58
  179.2 1.3 collective-permute-start.1
  180.5 3.0 collective-permute-start
  185.0 1.8 fusion.34
  189.8 16.5 %reduce-scatter.3.cloned.1.call-done = f32[32,2,8,128]{3,2,1,0:T(8,128)} async-done(((f32[128,2,8,128]{3,2,1,0:T(8,128)}), f32[32,2,8,128]{3,2,1,0:T(8,128)}) %reduce-scatter.3.cloned.1.call-update) | async-done | bytes 262160 | tf_op jit(solution)/shard_map/reduce_scatter | solution.py:111
  206.4 1.8 multiply_add_fusion
  208.1 54.9 %all-reduce.3.cloned.1.call-done = f32[128,128]{0,1:T(8,128)} async-done(((f32[128,128]{0,1:T(8,128)}), f32[128,128]{0,1:T(8,128)}) %all-reduce.3.cloned.1.call-update) | async-done | bytes 65552 | tf_op jit(solution)/shard_map/psum | solution.py:74
  263.0 51.2 %reduce-scatter.5.cloned.1.call-done = f32[16,8192]{1,0:T(8,128)} async-done(((f32[128,8192]{1,0:T(8,128)}), f32[16,8192]{1,0:T(8,128)}) %reduce-scatter.5.cloned.1.call-update) | async-done | bytes 524304 | tf_op jit(solution)/shard_map/reduce_scatter | solution.py:108
  314.2 2.9 fusion.8
  (169 shorter events, 66.0 us)
Async XLA Ops:
  7.2 34.3 %all-gather.2.cloned.1.call-start = ((), (), s32[]{:S(2)}) async-start(), calls=%async_computation.2 | async-start | bytes 2359296 | tf_op jit(solution)/shard_map/all_gather | solution.py:67
  7.9 198.5 %reduce-scatter.3.cloned.1.call-start = ((), (), s32[]{:S(2)}) async-start(), calls=%async_computation.3 | async-start | bytes 1310720 | tf_op jit(solution)/shard_map/reduce_scatter | solution.py:111
  177.8 1.2 copy-start.1
  179.0 4.6 %copy-start.2 = (s32[6,2,8,128]{3,2,1,0:T(8,128)S(1)}, s32[6,2,8,128]{3,2,1,0:T(8,128)}, u32[]{:S(2)}) copy-start(s32[6,2,8,128]{3,2,1,0:T(8,128)} %param.10) | copy-start | bytes 147460
  179.0 84.0 %all-reduce.3.cloned.1.call-start = ((), (), s32[]{:S(2)}) async-start(), calls=%async_computation.4 | async-start | bytes 131072 | tf_op jit(solution)/shard_map/psum | solution.py:74
  179.2 4.4 %collective-permute-start.1 = (bf16[128,1,8,128]{3,2,1,0:T(8,128)(2,1)S(1)}, bf16[128,1,8,128]{3,2,1,0:T(8,128)(2,1)S(1)}, u32[]{:S(2)}, u32[]{:S(2)}) collective-permute-start(bf16[128,1,8,128]{3,2,1,0:T(8,128)(2,1)S(1)} %get-tuple-element.170), channel_id=1, source_target_pairs={{4,0},{8,4},{12,8},{16,12},{20,16},{24,20},{28,24},{5,1},{9,5},{13... | collective-permute-start | bytes 786440 | tf_op jit(solution)/shard_map/ppermute | solution.py:19
  180.5 4.2 %collective-permute-start = (bf16[128,1,8,128]{3,2,1,0:T(8,128)(2,1)S(1)}, bf16[128,1,8,128]{3,2,1,0:T(8,128)(2,1)S(1)}, u32[]{:S(2)}, u32[]{:S(2)}) collective-permute-start(bf16[128,1,8,128]{3,2,1,0:T(8,128)(2,1)S(1)} %get-tuple-element.169), channel_id=1, source_target_pairs={{0,4},{4,8},{8,12},{12,16},{16,20},{20,24},{24,28},{1,5},{5,9},{9,... | collective-permute-start | bytes 786440 | tf_op jit(solution)/shard_map/ppermute | solution.py:17
  187.8 126.4 %reduce-scatter.5.cloned.1.call-start = ((), (), s32[]{:S(2)}) async-start(), calls=%async_computation.5 | async-start | bytes 4718592 | tf_op jit(solution)/shard_map/reduce_scatter | solution.py:108
  187.8 1.6 copy-start
Sparse Core Ops, SparseCore 0:
  9.6 31.7 all-gather.1
  179.1 27.2 reduce-scatter.2
  209.4 53.5 all-reduce.2
  265.1 48.9 reduce-scatter.4
where the time goes:
time: 326 us; the launch traced here: 324 us
  waiting for transfers between devices  144 us (44%)
  matrix products  111 us (34%)
  local copies, waits for them, and re-layouts  32.3 us (10%)
  between operations  13.9 us (4%)
  blocking collectives  11.8 us (4%)
  other arithmetic  5.54 us (2%)
  starting transfers between devices  4.5 us (1%)
    psum x1, waiting for transfers between devices, per_device(): moment = lax.psum(moment_part, 'space')  54.9 us
    reduce_scatter x1, waiting for transfers between devices, per_device(): l_proj = lax.psum_scatter(l_terms, 'space', scatter_dimension=0, tiled=True)  51.2 us
    dot_general x32, matrix products, tile_terms(): lax.dot_general(k_flat, v_block, (((0,), (0,)), ((), ())), preferred_elem...  50.6 us
    dot_general x32, matrix products, tile_terms(): lax.dot_general(v_block, reaction, (((1,), (1,)), ((), ())), preferred_el...  40.9 us
    dynamic_update_slice x64, local copies, waits for them, and re-layouts, turn_after(): l_terms = lax.dynamic_update_slice_in_dim(l_terms, l_term, offset, 1)  25 us
    all_gather x1, waiting for transfers between devices, per_device(): full_v = lax.all_gather(basis_v, 'space', axis=0, tiled=True)  18.8 us
    reduce_scatter x1, waiting for transfers between devices, per_device(): k_proj = lax.psum_scatter(k_term, 'samp', scatter_dimension=0, tiled=True)  16.5 us
    dot_general x32, matrix products, tile_terms(): lax.dot_general(u_rows, reaction, (((1,), (0,)), ((), ())), preferred_ele...  13.9 us
  transfers between devices with their start and end apart: 6, of which 5 were waited for; matrix products, arithmetic and copies ran while one was open for 3% of the time, Pallas kernels for 0%

commit v1 on v0

v1 whole, which is shorter than its diff:
```python
import functools

import jax
import jax.numpy as jnp
from jax import lax
from jax.experimental import pallas as pl
from jax.experimental.pallas import tpu as pltpu
from jax.sharding import PartitionSpec as P

step_size = 0.1
f32 = jnp.float32
bf16 = jnp.bfloat16


def dot(a, b, dims):
    return lax.dot_general(a, b, (dims, ((), ())), preferred_element_type=f32)


def joined(blocks):
    n, rows, columns = blocks.shape
    if rows % 16 == 0:
        return blocks.reshape(n * rows, columns)
    return blocks.astype(f32).reshape(n * rows, columns).astype(blocks.dtype)


def kernel(
    dims, u_ref, v_ref, core_ref, core_cols_ref, weight_ref, class_ref,
    k_out, l_out,
    u_all, v_all, k_rows, k_mine, halo_lo, halo_hi, lap, k_acc, react,
    m_parts, m_all, m_full, l_part, l_sib, l_sum, l_recv, k_part, k_recv,
    u_s, u_r, v_s, v_r, w_s, w_r, h_s, h_r, m_s, m_r, n_s, n_r,
    a_s, a_r, b_s, b_r, c_s, c_r,
):
    n_space, n_samp, n_chunks, chunk, tile, cell_tile, depth_x, rows_y, cols_z = dims
    n_chip = n_space // 2
    narrow, cells = u_ref.shape
    lane_width, samples = v_ref.shape
    rank = n_samp * narrow
    plane = rows_y * cols_z
    cell_scale = step_size * rank / (cells * n_space)
    samp_scale = rank / (samples * n_samp)

    me = lax.axis_index("space")
    col = lax.axis_index("samp")
    chip, core = me // 2, me % 2
    other = 1 - core

    def space_peer(k):
        return lax.rem(me + k, n_space)

    def samp_peer(k):
        return lax.rem(col + k, n_samp)

    def chip_peer(k):
        return lax.rem(chip + k, n_chip)

    def chip_before(k):
        return lax.rem(chip - k + n_chip, n_chip)

    def remote(src, dst, send, recv, where):
        return pltpu.make_async_remote_copy(
            src_ref=src, dst_ref=dst, send_sem=send, recv_sem=recv,
            device_id=where, device_id_type=pl.DeviceIdType.MESH,
        )

    def at_chunk(c):
        return pl.ds(pl.multiple_of(c * chunk, chunk), chunk)

    def to_sibling():
        return {"space": chip * 2 + other}

    def u_copy(k, slot):
        return remote(u_ref, u_all.at[slot], u_s.at[k], u_r.at[k], {"samp": samp_peer(k)})

    def v_copy(k, c, slot):
        return remote(
            v_ref.at[:, at_chunk(c)], v_all.at[slot, :, at_chunk(c)],
            v_s.at[k, c], v_r.at[k, c], {"space": chip_peer(k) * 2 + core},
        )

    def v_own(c, slot):
        return remote(
            v_ref.at[:, at_chunk(c)], v_all.at[slot, :, at_chunk(c)],
            w_s.at[0, c], w_r.at[0, c], to_sibling(),
        )

    def v_forward(k, c, slot):
        return remote(
            v_all.at[slot, :, at_chunk(c)], v_all.at[slot, :, at_chunk(c)],
            w_s.at[k, c], w_r.at[k, c], to_sibling(),
        )

    def l_swap(c):
        return remote(
            l_part.at[other, :, :, at_chunk(c)], l_sib.at[:, :, at_chunk(c)],
            a_s.at[c], a_r.at[c], to_sibling(),
        )

    def l_copy(k, c):
        return remote(
            l_sum.at[chip_peer(k), :, at_chunk(c)], l_recv.at[k - 1, :, at_chunk(c)],
            b_s.at[k, c], b_r.at[k, c], {"space": chip_peer(k) * 2 + core},
        )

    def m_copy(k, slot):
        return remote(m_parts.at[me], m_parts.at[slot], m_s.at[k], m_r.at[k], {"space": space_peer(k)})

    def m_share(k, slot):
        return remote(m_all.at[col], m_all.at[slot], n_s.at[k], n_r.at[k], {"samp": samp_peer(k)})

    def k_copy(k):
        return remote(k_part.at[samp_peer(k)], k_recv.at[k - 1], c_s.at[k], c_r.at[k], {"samp": samp_peer(k)})

    def halo_up():
        return remote(k_mine.at[:, pl.ds(cells - plane, plane)], halo_lo, h_s.at[0], h_r.at[0], {"space": space_peer(1)})

    def halo_down():
        return remote(k_mine.at[:, pl.ds(0, plane)], halo_hi, h_s.at[1], h_r.at[1], {"space": space_peer(n_space - 1)})

    barrier = pltpu.get_barrier_semaphore()
    for k in range(1, n_space):
        pl.semaphore_signal(barrier, inc=1, device_id={"space": space_peer(k)}, device_id_type=pl.DeviceIdType.MESH)
    for k in range(1, n_samp):
        pl.semaphore_signal(barrier, inc=1, device_id={"samp": samp_peer(k)}, device_id_type=pl.DeviceIdType.MESH)
    pl.semaphore_wait(barrier, n_space + n_samp - 2)

    for k in range(1, n_samp):
        u_copy(k, col).start()

    def send_v(c, carry):
        for k in range(1, n_chip):
            v_copy(k, c, me).start()
        v_own(c, me).start()
        return carry

    lax.fori_loop(0, n_chunks, send_v, 0)

    u_all[col] = u_ref[...]
    v_all[me] = v_ref[...]
    k_acc[...] = jnp.zeros_like(k_acc)

    for k in range(1, n_samp):
        u_copy(k, lax.rem(col - k + n_samp, n_samp)).wait_recv()

    core_b = core_ref[...].astype(bf16)
    for first in range(0, cells, cell_tile):
        spot = slice(first, first + cell_tile)
        u_tile = joined(u_all[:, :, spot])
        k_rows[spot, :] = dot(u_tile, core_b, ((0,), (0,))).astype(bf16)
        k_mine[:, spot] = dot(core_cols_ref[...], u_tile, ((1,), (0,))).astype(bf16)

    @pl.when(me < n_space - 1)
    def _():
        halo_up().start()

    @pl.when(me > 0)
    def _():
        halo_down().start()

    def forward(c):
        for k in range(1, n_chip):
            slot = chip_before(k) * 2 + core
            v_copy(k, c, slot).wait_recv()
            v_forward(k, c, slot).start()

    def await_sibling(c):
        v_own(c, chip * 2 + other).wait_recv()
        for k in range(1, n_chip):
            v_forward(k, c, chip_before(k) * 2 + other).wait_recv()

    def compute(c, part):
        spot = pl.ds(pl.multiple_of(c * chunk + part * tile, tile), tile)
        v = joined(v_all[:, :, spot])
        growth = 0.5 + 0.5 * class_ref[:, spot].astype(f32)
        for first in range(0, cells, cell_tile):
            rows = slice(first, first + cell_tile)
            field = dot(k_rows[rows, :], v, ((1,), (0,)))
            reaction = (field * (growth - field * field)).astype(bf16)
            react[rows, :] = reaction
            k_acc[rows, :] += dot(reaction, v, ((1,), (1,)))
        u_full = joined(u_all[...])
        onto_u = dot(u_full, react[...], ((1,), (0,))).astype(bf16)
        for place in range(n_chip):
            for side in range(2):
                row = (2 * place + side) * lane_width
                l_part[side, place, :, spot] = onto_u[row:row + lane_width, :]

    def chip_sum(c):
        l_swap(c).wait_recv()
        spot = at_chunk(c)
        l_sum[:, :, spot] = (l_part[core, :, :, spot].astype(f32) + l_sib[:, :, spot].astype(f32)).astype(bf16)
        for k in range(1, n_chip):
            l_copy(k, c).start()

    def stencil():
        @pl.when(me > 0)
        def _():
            halo_up().wait_recv()

        @pl.when(me == 0)
        def _():
            halo_lo[...] = jnp.zeros_like(halo_lo)

        @pl.when(me < n_space - 1)
        def _():
            halo_down().wait_recv()

        @pl.when(me == n_space - 1)
        def _():
            halo_hi[...] = jnp.zeros_like(halo_hi)

        lane = lax.broadcasted_iota(jnp.int32, (narrow, cols_z), 1)
        nothing = jnp.zeros((narrow, cols_z), f32)

        def line(ref, first):
            return ref[:, first:first + cols_z].astype(f32)

        for x in range(depth_x):
            for y in range(rows_y):
                at = (x * rows_y + y) * cols_z
                centre = line(k_mine, at)
                beside = (
                    line(k_mine, at - plane) if x > 0 else line(halo_lo, y * cols_z),
                    line(k_mine, at + plane) if x < depth_x - 1 else line(halo_hi, y * cols_z),
                    line(k_mine, at - cols_z) if y > 0 else nothing,
                    line(k_mine, at + cols_z) if y < rows_y - 1 else nothing,
                    jnp.where(lane == 0, 0.0, pltpu.roll(centre, 1, 1)),
                    jnp.where(lane == cols_z - 1, 0.0, pltpu.roll(centre, cols_z - 1, 1)),
                )
                summed = nothing
                for face in range(6):
                    summed = summed + weight_ref[face:face + 1, at:at + cols_z] * (beside[face] - centre)
                lap[:, at:at + cols_z] = summed
        m_parts[me] = dot(lap[...].astype(bf16), joined(u_all[...]), ((1,), (1,)))
        for k in range(1, n_space):
            m_copy(k, me).start()

    def moment_sum():
        for k in range(1, n_space):
            m_copy(k, lax.rem(me - k + n_space, n_space)).wait_recv()
        total = m_parts[0]
        for k in range(1, n_space):
            total = total + m_parts[k]
        m_all[col] = total
        for k in range(1, n_samp):
            m_share(k, col).start()

    def moment_rows():
        for k in range(1, n_samp):
            m_share(k, lax.rem(col - k + n_samp, n_samp)).wait_recv()
        moment = m_all[...].reshape(rank, rank).T
        m_full[...] = core_ref[...].astype(bf16).astype(f32) + cell_scale * moment

    def finish_l(c):
        spot = at_chunk(c)
        for k in range(1, n_chip):
            l_copy(k, c).wait_recv()
        total = l_sum[chip, :, spot].astype(f32)
        for k in range(1, n_chip):
            total = total + l_recv[k - 1, :, spot].astype(f32)
        mine = m_full[pl.ds(pl.multiple_of(me * lane_width, lane_width), lane_width), :]
        high = mine.astype(bf16)
        low = (mine - high.astype(f32)).astype(bf16)
        v = joined(v_all[:, :, spot])
        l_out[:, spot] = dot(high, v, ((1,), (0,))) + dot(low, v, ((1,), (0,))) + cell_scale * total

    forward(0)
    await_sibling(0)
    parts = chunk // tile

    def step(c, carry):
        compute(c, 0)

        @pl.when(c + 1 < n_chunks)
        def _():
            forward(c + 1)

        @pl.when(c > 0)
        def _():
            chip_sum(c - 1)

        for part in range(1, parts):
            compute(c, part)
        l_swap(c).start()

        for place, task in enumerate((stencil, moment_sum, moment_rows)):
            pl.when(c == min(place, n_chunks - 1))(task)

        @pl.when(c > 1)
        def _():
            finish_l(c - 2)

        @pl.when(c + 1 < n_chunks)
        def _():
            await_sibling(c + 1)

        return carry

    lax.fori_loop(0, n_chunks, step, 0)

    for first in range(0, cells, cell_tile):
        spot = slice(first, first + cell_tile)
        turned = (k_acc[spot, :].T * samp_scale).astype(bf16)
        for place in range(n_samp):
            k_part[place, :, spot] = turned[place * narrow:(place + 1) * narrow, :]
    for k in range(1, n_samp):
        k_copy(k).start()
    chip_sum(n_chunks - 1)
    if n_chunks > 1:
        finish_l(n_chunks - 2)
    for k in range(1, n_samp):
        k_copy(k).wait_recv()
    total = k_part[col].astype(f32)
    for k in range(1, n_samp):
        total = total + k_recv[k - 1].astype(f32)
    k_out[...] = k_mine[...].astype(f32) + step_size * (lap[...] + total)
    finish_l(n_chunks - 1)

    for k in range(1, n_samp):
        u_copy(k, col).wait_send()
        m_share(k, col).wait_send()
        k_copy(k).wait_send()
    for k in range(1, n_space):
        m_copy(k, me).wait_send()

    @pl.when(me < n_space - 1)
    def _():
        halo_up().wait_send()

    @pl.when(me > 0)
    def _():
        halo_down().wait_send()

    def sent(c, carry):
        for k in range(1, n_chip):
            v_copy(k, c, me).wait_send()
            v_forward(k, c, chip_before(k) * 2 + core).wait_send()
            l_copy(k, c).wait_send()
        v_own(c, me).wait_send()
        l_swap(c).wait_send()
        return carry

    lax.fori_loop(0, n_chunks, sent, 0)


def per_device(basis_u, basis_v, core_s, face_class, sample_class):
    n_space = lax.axis_size("space")
    n_samp = lax.axis_size("samp")
    narrow, depth_x, rows_y, cols_z = basis_u.shape
    rank = core_s.shape[0]
    lane_width, samples = basis_v.shape
    cells = depth_x * rows_y * cols_z
    plane = rows_y * cols_z
    n_chip = n_space // 2
    chunk = min(1024, samples)
    tile = min(512, chunk)
    cell_tile = min(512, cells)
    n_chunks = samples // chunk
    core_cols = lax.dynamic_slice_in_dim(
        core_s.astype(bf16).T, lax.axis_index("samp") * narrow, narrow, 0
    )
    weight = 0.25 * jnp.exp2(face_class.astype(f32)).reshape(face_class.shape[0], cells)
    dims = (n_space, n_samp, n_chunks, chunk, tile, cell_tile, depth_x, rows_y, cols_z)
    dma = pltpu.SemaphoreType.DMA
    vmem = pl.BlockSpec(memory_space=pltpu.VMEM)
    k_new, l_new = pl.pallas_call(
        functools.partial(kernel, dims),
        out_shape=(
            jax.ShapeDtypeStruct((narrow, cells), f32),
            jax.ShapeDtypeStruct((lane_width, samples), f32),
        ),
        in_specs=[vmem] * 6,
        out_specs=(vmem, vmem),
        scratch_shapes=[
            pltpu.VMEM((n_samp, narrow, cells), bf16),
            pltpu.VMEM((n_space, lane_width, samples), bf16),
            pltpu.VMEM((cells, rank), bf16),
            pltpu.VMEM((narrow, cells), bf16),
            pltpu.VMEM((narrow, plane), bf16),
            pltpu.VMEM((narrow, plane), bf16),
            pltpu.VMEM((narrow, cells), f32),
            pltpu.VMEM((cells, rank), f32),
            pltpu.VMEM((cells, tile), bf16),
            pltpu.VMEM((n_space, narrow, rank), f32),
            pltpu.VMEM((n_samp, narrow, rank), f32),
            pltpu.VMEM((rank, rank), f32),
            pltpu.VMEM((2, n_chip, lane_width, samples), bf16),
            pltpu.VMEM((n_chip, lane_width, samples), bf16),
            pltpu.VMEM((n_chip, lane_width, samples), bf16),
            pltpu.VMEM((n_chip - 1, lane_width, samples), bf16),
            pltpu.VMEM((n_samp, narrow, cells), bf16),
            pltpu.VMEM((n_samp - 1, narrow, cells), bf16),
            dma((n_samp,)), dma((n_samp,)),
            dma((n_chip, n_chunks)), dma((n_chip, n_chunks)),
            dma((n_chip, n_chunks)), dma((n_chip, n_chunks)),
            dma((2,)), dma((2,)),
            dma((n_space,)), dma((n_space,)),
            dma((n_samp,)), dma((n_samp,)),
            dma((n_chunks,)), dma((n_chunks,)),
            dma((n_chip, n_chunks)), dma((n_chip, n_chunks)),
            dma((n_samp,)), dma((n_samp,)),
        ],
        compiler_params=pltpu.CompilerParams(
            collective_id=0, has_side_effects=True, vmem_limit_bytes=48 * 1024 * 1024
        ),
        cost_estimate=pl.CostEstimate(
            flops=6 * cells * samples * rank, bytes_accessed=2 * rank * samples, transcendentals=0
        ),
    )(
        basis_u.reshape(narrow, cells), basis_v, core_s, core_cols, weight,
        sample_class.reshape(1, samples),
    )
    return (k_new.reshape(narrow, depth_x, rows_y, cols_z), l_new)


def solution(mesh):
    placed = (
        P("samp", "space", None, None),
        P("space", "samp"),
        P(),
        P(None, "space", None, None),
        P("samp"),
    )
    return jax.shard_map(
        per_device,
        mesh=mesh,
        in_specs=placed,
        out_specs=(P("samp", "space", None, None), P("space", "samp")),
        check_vma=False,
    )
```

time: 326 us -> 73.4 us (0.23)
  waiting for transfers between devices: 144 us -> 0 us
  matrix products: 111 us -> 0 us
  Pallas kernels: 0 us -> 69 us
  local copies, waits for them, and re-layouts: 32.3 us -> 3.44 us
  between operations: 13.9 us -> 0.71 us
  blocking collectives: 11.8 us -> 0 us
  other arithmetic: 5.54 us -> 0.04 us
  starting transfers between devices: 4.5 us -> 0 us
    dot_general x100 -> x0, matrix products: 111 us -> none  [the longest x32 50.6 us: tile_terms(): lax.dot_general(k_flat, v_block, (((0,), (0,)), ((), ())), preferred_elem...]
    pallas_call x0 -> x1, Pallas kernels: none -> 69 us  [per_device(): pl.pallas_call(functools.partial(kernel, dims), out_shape=(jax.ShapeDtype...]
    reduce_scatter x2 -> x0, waiting for transfers between devices: 67.7 us -> none  [the longest x1 51.2 us: per_device(): l_proj = lax.psum_scatter(l_terms, 'space', scatter_dimension=0, tiled=True)]
    psum x1 -> x0, waiting for transfers between devices: 54.9 us -> none  [per_device(): moment = lax.psum(moment_part, 'space')]
    dynamic_update_slice x64 -> x0, local copies, waits for them, and re-layouts: 25 us -> none  [turn_after(): l_terms = lax.dynamic_update_slice_in_dim(l_terms, l_term, offset, 1)]
    all_gather x1 -> x0, waiting for transfers between devices: 18.8 us -> none  [per_device(): full_v = lax.all_gather(basis_v, 'space', axis=0, tiled=True)]
    all_gather x1 -> x0, blocking collectives: 11.8 us -> none  [per_device(): full_u = lax.all_gather(basis_u, 'samp', axis=0, tiled=True)]
    ppermute x2 -> x0, starting transfers between devices: 4.34 us -> none  [the longest x1 3.05 us: padded(): lax.ppermute(tail, axis, [(i, (i + 1) % count) for i in range(ends)])]
  transfers between devices with their start and end apart: 6 -> 0, of which waited for: 5 -> 0; matrix products, arithmetic and copies ran while one was open for 3% -> 0% of each run, Pallas kernels for 0% -> 0%
where the time goes in v1:
time: 73.4 us; the launch traced here: 73.2 us
  Pallas kernels  69 us (94%)
  local copies, waits for them, and re-layouts  3.44 us (5%)
    pallas_call x1, Pallas kernels, per_device(): pl.pallas_call(functools.partial(kernel, dims), out_shape=(jax.ShapeDtype...  69 us
    unnamed x15, local copies, waits for them, and re-layouts  2.48 us

profile of v1, /device:TPU:0, one launch (start us, length us, event | category | flops | bytes accessed | tf_op | source)
XLA Modules:
  0.0 73.2 jit_solution(10960000324289938552)
XLA Ops:
  0.6 0.0 copy-start.4
  0.6 0.0 copy-start.3
  0.7 1.0 %constant_dynamic-slice_fusion = bf16[128,32]{1,0:T(8,128)(2,1)S(1)} fusion(f32[128,128]{1,0:T(8,128)} %core_ref.1, s32[]{:T(128)S(6)} %select_n.3), kind=kLoop, calls=%fused_computation.4 | loop fusion | bytes 16388 | tf_op jit(solution)/shard_map/dynamic-slice
  1.6 0.0 copy-start.1
  1.6 0.1 copy.8
  1.7 0.0 copy-done.4
  1.8 0.0 copy-done.3
  1.8 0.0 copy-start
  1.8 0.0 copy-start.2
  1.8 0.7 copy-done.1
  2.6 0.1 copy-done
  2.6 0.0 copy-done.2
  2.6 69.0 %shard_map.68 = (f32[32,2048]{1,0:T(8,128)S(1)}, f32[16,8192]{1,0:T(8,128)S(1)}) custom-call(bf16[32,2048]{1,0:T(8,128)(2,1)S(1)} %bitcast.19, bf16[16,8192]{1,0:T(8,128)(2,1)S(1)} %copy-done.1, f32[128,128]{1,0:T(8,128)S(1)} %copy-done, bf16[32,128]{1,0:T(8,128)(2,1)S(1)} %bitcast.21, f32[6,2048]{1,0:T(8,128)S(1)} %bitcast.20, s32[1,8192]{1,0:T(1,128)S(1)} %bitcast.22), custom_call_target="tpu_custom_call" | custom-call | flops 12884901888 | bytes 2097152 | tf_op jit(solution)/shard_map/pallas_call | solution.py:366
  71.7 0.8 %copy.11 = f32[4,8,16,128]{3,2,1,0:T(8,128)} copy(f32[4,8,16,128]{3,1,2,0:T(8,128)S(1)} %bitcast.18) | data formatting | bytes 524288
  72.4 0.8 %copy.17 = f32[16,8192]{1,0:T(8,128)} copy(f32[16,8192]{1,0:T(8,128)S(1)} %get-tuple-element.9) | data formatting | bytes 1048576
  (3 shorter events, 0.1 us)
Async XLA Ops:
  0.6 1.0 %copy-start.4 = (s32[6,2,8,128]{3,2,1,0:T(8,128)S(1)}, s32[6,2,8,128]{3,2,1,0:T(8,128)}, u32[]{:S(2)}) copy-start(s32[6,2,8,128]{3,2,1,0:T(8,128)} %param.8) | copy-start | bytes 147460
  0.6 1.1 %copy-start.3 = (bf16[32,2,8,128]{3,2,1,0:T(8,128)(2,1)S(1)}, bf16[32,2,8,128]{3,2,1,0:T(8,128)(2,1)}, u32[]{:S(2)}) copy-start(bf16[32,2,8,128]{3,2,1,0:T(8,128)(2,1)} %param.5) | copy-start | bytes 393220
  1.6 1.0 %copy-start.1 = (bf16[16,8192]{1,0:T(8,128)(2,1)S(1)}, bf16[16,8192]{1,0:T(8,128)(2,1)}, u32[]{:S(2)}) copy-start(bf16[16,8192]{1,0:T(8,128)(2,1)} %v_ref.1) | copy-start | bytes 786436
  1.8 0.9 %copy-start = (f32[128,128]{1,0:T(8,128)S(1)}, f32[128,128]{1,0:T(8,128)}, u32[]{:S(2)}) copy-start(f32[128,128]{1,0:T(8,128)} %core_ref.1) | copy-start | bytes 196612
  1.8 0.9 %copy-start.2 = (s32[8192]{0:T(1024)S(1)}, s32[8192]{0:T(1024)}, u32[]{:S(2)}) copy-start(s32[8192]{0:T(1024)} %param.9) | copy-start | bytes 98308

commit v2 on v1

--- a/solution.py
+++ b/solution.py
@@ -27,12 +27,13 @@
     dims, u_ref, v_ref, core_ref, core_cols_ref, weight_ref, class_ref,
     k_out, l_out,
     u_all, v_all, k_rows, k_mine, halo_lo, halo_hi, lap, k_acc, react,
-    m_parts, m_all, m_full, l_part, l_sib, l_sum, l_recv, k_part, k_recv,
+    m_parts, m_all, m_full, l_part, l_sib, l_sum, l_recv, l_out_line, l_in_line, k_part, k_recv,
     u_s, u_r, v_s, v_r, w_s, w_r, h_s, h_r, m_s, m_r, n_s, n_r,
-    a_s, a_r, b_s, b_r, c_s, c_r,
+    a_s, a_r, b_s, b_r, c_s, c_r, d_s, d_r,
 ):
     n_space, n_samp, n_chunks, chunk, tile, cell_tile, depth_x, rows_y, cols_z = dims
     n_chip = n_space // 2
+    n_line = max(0, n_chunks - 2)
     narrow, cells = u_ref.shape
     lane_width, samples = v_ref.shape
     rank = n_samp * narrow
@@ -72,22 +73,47 @@
     def u_copy(k, slot):
         return remote(u_ref, u_all.at[slot], u_s.at[k], u_r.at[k], {"samp": samp_peer(k)})
 
-    def v_copy(k, c, slot):
+    def toward(side):
+        return lax.rem(chip + (1 if side == 0 else n_chip - 1), n_chip)
+
+    def held(side, k):
+        return chip >= k if side == 0 else chip + k < n_chip
+
+    def goes_on(side):
+        return chip < n_chip - 1 if side == 0 else chip > 0
+
+    def origin(side, k):
+        return lax.rem(chip + (n_chip - k if side == 0 else k), n_chip)
+
+    def v_line(side, k, c):
+        slot = origin(side, k) * 2 + core
+        block = v_all.at[slot, :, at_chunk(c)]
         return remote(
-            v_ref.at[:, at_chunk(c)], v_all.at[slot, :, at_chunk(c)],
-            v_s.at[k, c], v_r.at[k, c], {"space": chip_peer(k) * 2 + core},
+            v_ref.at[:, at_chunk(c)] if k == 0 else block, block,
+            v_s.at[side, k, c], v_r.at[side, k + 1, c], {"space": toward(side) * 2 + core},
+        )
+
+    def v_arrival(side, k, c):
+        block = v_all.at[origin(side, k) * 2 + core, :, at_chunk(c)]
+        return remote(
+            block, block, v_s.at[side, k - 1, c], v_r.at[side, k, c],
+            {"space": toward(side) * 2 + core},
         )
 
     def v_own(c, slot):
         return remote(
             v_ref.at[:, at_chunk(c)], v_all.at[slot, :, at_chunk(c)],
-            w_s.at[0, c], w_r.at[0, c], to_sibling(),
-        )
-
-    def v_forward(k, c, slot):
+            w_s.at[0, 0, c], w_r.at[0, 0, c], to_sibling(),
+        )
+
+    def v_forward(side, k, c, which):
+        block = v_all.at[origin(side, k) * 2 + which, :, at_chunk(c)]
+        return remote(block, block, w_s.at[side, k, c], w_r.at[side, k, c], to_sibling())
+
+    def l_line(side, target, c):
         return remote(
-            v_all.at[slot, :, at_chunk(c)], v_all.at[slot, :, at_chunk(c)],
-            w_s.at[k, c], w_r.at[k, c], to_sibling(),
+            l_out_line.at[side, target, :, at_chunk(c)], l_in_line.at[side, target, :, at_chunk(c)],
+            d_s.at[side, target, c], d_r.at[side, target, c], {"space": toward(side) * 2 + core},
         )
 
     def l_swap(c):
@@ -127,17 +153,40 @@
     for k in range(1, n_samp):
         u_copy(k, col).start()
 
-    def send_v(c, carry):
-        for k in range(1, n_chip):
-            v_copy(k, c, me).start()
-        v_own(c, me).start()
-        return carry
-
-    lax.fori_loop(0, n_chunks, send_v, 0)
-
+    def wave(w):
+        for k in range(n_chip):
+            c = w - k
+
+            @pl.when((c >= 0) & (c < n_chunks))
+            def _():
+                for side in range(2):
+                    if k > 0:
+                        @pl.when(held(side, k))
+                        def _():
+                            v_arrival(side, k, c).wait_recv()
+
+                            @pl.when(goes_on(side))
+                            def _():
+                                v_line(side, k, c).start()
+
+                            v_forward(side, k, c, core).start()
+                    else:
+                        @pl.when(goes_on(side))
+                        def _():
+                            v_line(side, k, c).start()
+                if k == 0:
+                    v_own(c, me).start()
+
+    wave(0)
     u_all[col] = u_ref[...]
     v_all[me] = v_ref[...]
     k_acc[...] = jnp.zeros_like(k_acc)
+    for side in range(2):
+        @pl.when(chip == (0 if side == 0 else n_chip - 1))
+        def _():
+            l_in_line[side] = jnp.zeros_like(l_in_line[side])
+    wave(1)
+    wave(2)
 
     for k in range(1, n_samp):
         u_copy(k, lax.rem(col - k + n_samp, n_samp)).wait_recv()
@@ -157,16 +206,13 @@
     def _():
         halo_down().start()
 
-    def forward(c):
-        for k in range(1, n_chip):
-            slot = chip_before(k) * 2 + core
-            v_copy(k, c, slot).wait_recv()
-            v_forward(k, c, slot).start()
-
     def await_sibling(c):
         v_own(c, chip * 2 + other).wait_recv()
-        for k in range(1, n_chip):
-            v_forward(k, c, chip_before(k) * 2 + other).wait_recv()
+        for side in range(2):
+            for k in range(1, n_chip):
+                @pl.when(held(side, k))
+                def _():
+                    v_forward(side, k, c, other).wait_recv()
 
     def compute(c, part):
         spot = pl.ds(pl.multiple_of(c * chunk + part * tile, tile), tile)
@@ -189,8 +235,30 @@
         l_swap(c).wait_recv()
         spot = at_chunk(c)
         l_sum[:, :, spot] = (l_part[core, :, :, spot].astype(f32) + l_sib[:, :, spot].astype(f32)).astype(bf16)
-        for k in range(1, n_chip):
-            l_copy(k, c).start()
+
+        @pl.when(c >= n_line)
+        def _():
+            for k in range(1, n_chip):
+                l_copy(k, c).start()
+
+    def line_sums(t):
+        for side in range(2):
+            c = t - 1 - (chip if side == 0 else n_chip - 1 - chip)
+
+            @pl.when((c >= 0) & (c < n_line))
+            def _():
+                spot = at_chunk(c)
+                for target in range(n_chip):
+                    @pl.when(chip < target if side == 0 else chip > target)
+                    def _():
+                        @pl.when(chip > 0 if side == 0 else chip < n_chip - 1)
+                        def _():
+                            l_line(side, target, c).wait_recv()
+
+                        l_out_line[side, target, :, spot] = (
+                            l_sum[target, :, spot].astype(f32) + l_in_line[side, target, :, spot].astype(f32)
+                        ).astype(bf16)
+                        l_line(side, target, c).start()
 
     def stencil():
         @pl.when(me > 0)
@@ -251,34 +319,43 @@
         moment = m_all[...].reshape(rank, rank).T
         m_full[...] = core_ref[...].astype(bf16).astype(f32) + cell_scale * moment
 
-    def finish_l(c):
+    def finish_with(c, terms):
         spot = at_chunk(c)
-        for k in range(1, n_chip):
-            l_copy(k, c).wait_recv()
         total = l_sum[chip, :, spot].astype(f32)
-        for k in range(1, n_chip):
-            total = total + l_recv[k - 1, :, spot].astype(f32)
+        for term in terms:
+            total = total + term[:, spot].astype(f32)
         mine = m_full[pl.ds(pl.multiple_of(me * lane_width, lane_width), lane_width), :]
         high = mine.astype(bf16)
         low = (mine - high.astype(f32)).astype(bf16)
         v = joined(v_all[:, :, spot])
         l_out[:, spot] = dot(high, v, ((1,), (0,))) + dot(low, v, ((1,), (0,))) + cell_scale * total
 
-    forward(0)
+    def finish_direct(c):
+        for k in range(1, n_chip):
+            l_copy(k, c).wait_recv()
+        finish_with(c, [l_recv.at[k - 1] for k in range(1, n_chip)])
+
+    def finish_line(c):
+        for side in range(2):
+            @pl.when(chip > 0 if side == 0 else chip < n_chip - 1)
+            def _():
+                l_line(side, chip, c).wait_recv()
+        finish_with(c, [l_in_line.at[side, chip] for side in range(2)])
+
+    for w in range(3, n_chip):
+        wave(w)
     await_sibling(0)
     parts = chunk // tile
 
     def step(c, carry):
         compute(c, 0)
-
-        @pl.when(c + 1 < n_chunks)
-        def _():
-            forward(c + 1)
+        wave(c + n_chip)
 
         @pl.when(c > 0)
         def _():
             chip_sum(c - 1)
 
+        line_sums(c)
         for part in range(1, parts):
             compute(c, part)
         l_swap(c).start()
@@ -286,9 +363,9 @@
         for place, task in enumerate((stencil, moment_sum, moment_rows)):
             pl.when(c == min(place, n_chunks - 1))(task)
 
-        @pl.when(c > 1)
-        def _():
-            finish_l(c - 2)
+        @pl.when((c >= n_chip) & (c - n_chip < n_line))
+        def _():
+            finish_line(c - n_chip)
 
         @pl.when(c + 1 < n_chunks)
         def _():
@@ -306,15 +383,19 @@
     for k in range(1, n_samp):
         k_copy(k).start()
     chip_sum(n_chunks - 1)
-    if n_chunks > 1:
-        finish_l(n_chunks - 2)
+    for t in range(n_chunks, n_line + n_chip):
+        line_sums(t)
+    for c in range(max(0, n_chunks - n_chip), n_line):
+        finish_line(c)
+    for c in range(n_line, n_chunks - 1):
+        finish_direct(c)
     for k in range(1, n_samp):
         k_copy(k).wait_recv()
     total = k_part[col].astype(f32)
     for k in range(1, n_samp):
         total = total + k_recv[k - 1].astype(f32)
     k_out[...] = k_mine[...].astype(f32) + step_size * (lap[...] + total)
-    finish_l(n_chunks - 1)
+    finish_direct(n_chunks - 1)
 
     for k in range(1, n_samp):
         u_copy(k, col).wait_send()
@@ -332,12 +413,32 @@
         halo_down().wait_send()
 
     def sent(c, carry):
-        for k in range(1, n_chip):
-            v_copy(k, c, me).wait_send()
-            v_forward(k, c, chip_before(k) * 2 + core).wait_send()
-            l_copy(k, c).wait_send()
+        for side in range(2):
+            for k in range(n_chip):
+                @pl.when(held(side, k) & goes_on(side))
+                def _():
+                    v_line(side, k, c).wait_send()
+
+                if k > 0:
+                    @pl.when(held(side, k))
+                    def _():
+                        v_forward(side, k, c, core).wait_send()
         v_own(c, me).wait_send()
         l_swap(c).wait_send()
+
+        @pl.when(c < n_line)
+        def _():
+            for side in range(2):
+                for target in range(n_chip):
+                    @pl.when(chip < target if side == 0 else chip > target)
+                    def _():
+                        l_line(side, target, c).wait_send()
+
+        @pl.when(c >= n_line)
+        def _():
+            for k in range(1, n_chip):
+                l_copy(k, c).wait_send()
+
         return carry
 
     lax.fori_loop(0, n_chunks, sent, 0)
@@ -388,17 +489,20 @@
             pltpu.VMEM((n_chip, lane_width, samples), bf16),
             pltpu.VMEM((n_chip, lane_width, samples), bf16),
             pltpu.VMEM((n_chip - 1, lane_width, samples), bf16),
+            pltpu.VMEM((2, n_chip, lane_width, samples), bf16),
+            pltpu.VMEM((2, n_chip, lane_width, samples), bf16),
             pltpu.VMEM((n_samp, narrow, cells), bf16),
             pltpu.VMEM((n_samp - 1, narrow, cells), bf16),
             dma((n_samp,)), dma((n_samp,)),
-            dma((n_chip, n_chunks)), dma((n_chip, n_chunks)),
-            dma((n_chip, n_chunks)), dma((n_chip, n_chunks)),
+            dma((2, n_chip, n_chunks)), dma((2, n_chip + 1, n_chunks)),
+            dma((2, n_chip, n_chunks)), dma((2, n_chip, n_chunks)),
             dma((2,)), dma((2,)),
             dma((n_space,)), dma((n_space,)),
             dma((n_samp,)), dma((n_samp,)),
             dma((n_chunks,)), dma((n_chunks,)),
             dma((n_chip, n_chunks)), dma((n_chip, n_chunks)),
             dma((n_samp,)), dma((n_samp,)),
+            dma((2, n_chip, n_chunks)), dma((2, n_chip, n_chunks)),
         ],
         compiler_params=pltpu.CompilerParams(
             collective_id=0, has_side_effects=True, vmem_limit_bytes=48 * 1024 * 1024

time: 73.4 us -> 65.3 us (0.89)
  Pallas kernels: 69 us -> 61 us
    pallas_call x1, Pallas kernels: 69 us -> 61 us  [per_device(): pl.pallas_call(functools.partial(kernel, dims), out_shape=(jax.ShapeDtype...]
where the time goes in v2:
time: 65.3 us; the launch traced here: 65.2 us
  Pallas kernels  61 us (93%)
  local copies, waits for them, and re-layouts  3.44 us (5%)
  between operations  0.71 us (1%)
    pallas_call x1, Pallas kernels, per_device(): pl.pallas_call(functools.partial(kernel, dims), out_shape=(jax.ShapeDtype...  61 us
    unnamed x15, local copies, waits for them, and re-layouts  2.48 us

profile of v2, /device:TPU:0, one launch (start us, length us, event | category | flops | bytes accessed | tf_op | source)
XLA Modules:
  0.0 65.2 jit_solution(1872027801564215511)
XLA Ops:
  0.6 0.0 copy-start.4
  0.6 0.0 copy-start.3
  0.7 1.0 %constant_dynamic-slice_fusion = bf16[128,32]{1,0:T(8,128)(2,1)S(1)} fusion(f32[128,128]{1,0:T(8,128)} %core_ref.1, s32[]{:T(128)S(6)} %select_n.3), kind=kLoop, calls=%fused_computation.4 | loop fusion | bytes 16388 | tf_op jit(solution)/shard_map/dynamic-slice
  1.6 0.0 copy-start.1
  1.6 0.1 copy.8
  1.7 0.0 copy-done.4
  1.8 0.0 copy-done.3
  1.8 0.0 copy-start
  1.8 0.0 copy-start.2
  1.8 0.7 %copy-done.1 = bf16[16,8192]{1,0:T(8,128)(2,1)S(1)} copy-done((bf16[16,8192]{1,0:T(8,128)(2,1)S(1)}, bf16[16,8192]{1,0:T(8,128)(2,1)}, u32[]{:S(2)}) %copy-start.1) | copy-done | bytes 262168
  2.6 0.1 copy-done
  2.6 0.0 copy-done.2
  2.6 61.0 %shard_map.68 = (f32[32,2048]{1,0:T(8,128)S(1)}, f32[16,8192]{1,0:T(8,128)S(1)}) custom-call(bf16[32,2048]{1,0:T(8,128)(2,1)S(1)} %bitcast.19, bf16[16,8192]{1,0:T(8,128)(2,1)S(1)} %copy-done.1, f32[128,128]{1,0:T(8,128)S(1)} %copy-done, bf16[32,128]{1,0:T(8,128)(2,1)S(1)} %bitcast.21, f32[6,2048]{1,0:T(8,128)S(1)} %bitcast.20, s32[1,8192]{1,0:T(1,128)S(1)} %bitcast.22), custom_call_target="tpu_custom_call" | custom-call | flops 12884901888 | bytes 2097152 | tf_op jit(solution)/shard_map/pallas_call | solution.py:467
  63.6 0.8 %copy.11 = f32[4,8,16,128]{3,2,1,0:T(8,128)} copy(f32[4,8,16,128]{3,1,2,0:T(8,128)S(1)} %bitcast.18) | data formatting | bytes 524288
  64.4 0.8 %copy.17 = f32[16,8192]{1,0:T(8,128)} copy(f32[16,8192]{1,0:T(8,128)S(1)} %get-tuple-element.9) | data formatting | bytes 1048576
  (3 shorter events, 0.1 us)
Async XLA Ops:
  0.6 1.0 %copy-start.4 = (s32[6,2,8,128]{3,2,1,0:T(8,128)S(1)}, s32[6,2,8,128]{3,2,1,0:T(8,128)}, u32[]{:S(2)}) copy-start(s32[6,2,8,128]{3,2,1,0:T(8,128)} %param.8) | copy-start | bytes 147460
  0.6 1.1 %copy-start.3 = (bf16[32,2,8,128]{3,2,1,0:T(8,128)(2,1)S(1)}, bf16[32,2,8,128]{3,2,1,0:T(8,128)(2,1)}, u32[]{:S(2)}) copy-start(bf16[32,2,8,128]{3,2,1,0:T(8,128)(2,1)} %param.5) | copy-start | bytes 393220
  1.6 1.0 %copy-start.1 = (bf16[16,8192]{1,0:T(8,128)(2,1)S(1)}, bf16[16,8192]{1,0:T(8,128)(2,1)}, u32[]{:S(2)}) copy-start(bf16[16,8192]{1,0:T(8,128)(2,1)} %v_ref.1) | copy-start | bytes 786436
  1.8 0.9 %copy-start = (f32[128,128]{1,0:T(8,128)S(1)}, f32[128,128]{1,0:T(8,128)}, u32[]{:S(2)}) copy-start(f32[128,128]{1,0:T(8,128)} %core_ref.1) | copy-start | bytes 196612
  1.8 0.9 %copy-start.2 = (s32[8192]{0:T(1024)S(1)}, s32[8192]{0:T(1024)}, u32[]{:S(2)}) copy-start(s32[8192]{0:T(1024)} %param.9) | copy-start | bytes 98308

commit v3 on v2

--- a/solution.py
+++ b/solution.py
@@ -360,7 +360,7 @@
             compute(c, part)
         l_swap(c).start()
 
-        for place, task in enumerate((stencil, moment_sum, moment_rows)):
+        for place, task in ((0, stencil), (2, moment_sum), (4, moment_rows)):
             pl.when(c == min(place, n_chunks - 1))(task)
 
         @pl.when((c >= n_chip) & (c - n_chip < n_line))

time: 65.3 us -> 64.3 us (0.985)
  Pallas kernels: 61 us -> 59.9 us
    pallas_call x1, Pallas kernels: 61 us -> 59.9 us  [per_device(): pl.pallas_call(functools.partial(kernel, dims), out_shape=(jax.ShapeDtype...]
where the time goes in v3:
time: 64.3 us; the launch traced here: 64.1 us
  Pallas kernels  59.9 us (93%)
  local copies, waits for them, and re-layouts  3.44 us (5%)
  between operations  0.71 us (1%)
    pallas_call x1, Pallas kernels, per_device(): pl.pallas_call(functools.partial(kernel, dims), out_shape=(jax.ShapeDtype...  59.9 us
    unnamed x15, local copies, waits for them, and re-layouts  2.48 us

profile of v3, /device:TPU:0, one launch (start us, length us, event | category | flops | bytes accessed | tf_op | source)
XLA Modules:
  0.0 64.1 jit_solution(2353178035323698391)
XLA Ops:
  0.6 0.0 copy-start.4
  0.6 0.0 copy-start.3
  0.7 1.0 %constant_dynamic-slice_fusion = bf16[128,32]{1,0:T(8,128)(2,1)S(1)} fusion(f32[128,128]{1,0:T(8,128)} %core_ref.1, s32[]{:T(128)S(6)} %select_n.3), kind=kLoop, calls=%fused_computation.4 | loop fusion | bytes 16388 | tf_op jit(solution)/shard_map/dynamic-slice
  1.6 0.0 copy-start.1
  1.6 0.1 copy.8
  1.7 0.0 copy-done.4
  1.8 0.0 copy-done.3
  1.8 0.0 copy-start
  1.8 0.0 copy-start.2
  1.8 0.7 %copy-done.1 = bf16[16,8192]{1,0:T(8,128)(2,1)S(1)} copy-done((bf16[16,8192]{1,0:T(8,128)(2,1)S(1)}, bf16[16,8192]{1,0:T(8,128)(2,1)}, u32[]{:S(2)}) %copy-start.1) | copy-done | bytes 262168
  2.6 0.1 copy-done
  2.6 0.0 copy-done.2
  2.6 59.9 %shard_map.68 = (f32[32,2048]{1,0:T(8,128)S(1)}, f32[16,8192]{1,0:T(8,128)S(1)}) custom-call(bf16[32,2048]{1,0:T(8,128)(2,1)S(1)} %bitcast.19, bf16[16,8192]{1,0:T(8,128)(2,1)S(1)} %copy-done.1, f32[128,128]{1,0:T(8,128)S(1)} %copy-done, bf16[32,128]{1,0:T(8,128)(2,1)S(1)} %bitcast.21, f32[6,2048]{1,0:T(8,128)S(1)} %bitcast.20, s32[1,8192]{1,0:T(1,128)S(1)} %bitcast.22), custom_call_target="tpu_custom_call" | custom-call | flops 12884901888 | bytes 2097152 | tf_op jit(solution)/shard_map/pallas_call | solution.py:467
  62.6 0.8 %copy.11 = f32[4,8,16,128]{3,2,1,0:T(8,128)} copy(f32[4,8,16,128]{3,1,2,0:T(8,128)S(1)} %bitcast.18) | data formatting | bytes 524288
  63.3 0.8 %copy.17 = f32[16,8192]{1,0:T(8,128)} copy(f32[16,8192]{1,0:T(8,128)S(1)} %get-tuple-element.9) | data formatting | bytes 1048576
  (3 shorter events, 0.1 us)
Async XLA Ops:
  0.6 1.0 %copy-start.4 = (s32[6,2,8,128]{3,2,1,0:T(8,128)S(1)}, s32[6,2,8,128]{3,2,1,0:T(8,128)}, u32[]{:S(2)}) copy-start(s32[6,2,8,128]{3,2,1,0:T(8,128)} %param.8) | copy-start | bytes 147460
  0.6 1.1 %copy-start.3 = (bf16[32,2,8,128]{3,2,1,0:T(8,128)(2,1)S(1)}, bf16[32,2,8,128]{3,2,1,0:T(8,128)(2,1)}, u32[]{:S(2)}) copy-start(bf16[32,2,8,128]{3,2,1,0:T(8,128)(2,1)} %param.5) | copy-start | bytes 393220
  1.6 1.0 %copy-start.1 = (bf16[16,8192]{1,0:T(8,128)(2,1)S(1)}, bf16[16,8192]{1,0:T(8,128)(2,1)}, u32[]{:S(2)}) copy-start(bf16[16,8192]{1,0:T(8,128)(2,1)} %v_ref.1) | copy-start | bytes 786436
  1.8 0.9 %copy-start = (f32[128,128]{1,0:T(8,128)S(1)}, f32[128,128]{1,0:T(8,128)}, u32[]{:S(2)}) copy-start(f32[128,128]{1,0:T(8,128)} %core_ref.1) | copy-start | bytes 196612
  1.8 0.9 %copy-start.2 = (s32[8192]{0:T(1024)S(1)}, s32[8192]{0:T(1024)}, u32[]{:S(2)}) copy-start(s32[8192]{0:T(1024)} %param.9) | copy-start | bytes 98308
